TPU v7x, 32 devices: a whole 2x2x4 slice. The times are simulated.
32 devices in a mesh: grp: 2 (over x), req: 16 (over z, y, core).
Axes of the slice: x: 2, y: 2, z: 4, core: 2. Of those that a mesh axis runs over, the one named last changes fastest.
Arguments:
- moe_input: bfloat16 [512, 2048], P(('grp', 'req')), parts along dimension 0, may hold values from -6 to 6
- norm_gain: bfloat16 [2048], replicated, may hold values from 0.25 to 1.75
- route_ids: int32 [512, 8], P(('grp', 'req')), parts along dimension 0, may hold values from 0 to 15, all different within a row; in each aligned block of 16 rows (0 to 15, 16 to 31, ...) at most 16 rows name the same one
- route_gates: bfloat16 [512, 8], P(('grp', 'req')), parts along dimension 0, may hold values from 0.049804688 to 0.5
- expert_gate: bfloat16 [16, 2048, 768], P('req'), may hold values from -0.125 to 0.125
- expert_up: bfloat16 [16, 2048, 768], P('req'), may hold values from -0.125 to 0.125
- expert_down: bfloat16 [16, 768, 2048], P('req'), may hold values from -0.21875 to 0.21875
- queries: bfloat16 [128, 4096], P(('grp', 'req')), parts along dimension 0, may hold values from -4.5 to 4.5
- keys_cache: bfloat16 [128, 4, 384, 128], P(('grp', 'req')), parts along dimension 0, may hold values from -4.5 to 4.5
- values_cache: bfloat16 [128, 4, 384, 128], P(('grp', 'req')), parts along dimension 0, may hold values from -4.5 to 4.5
- new_keys: bfloat16 [128, 512], P(('grp', 'req')), parts along dimension 0, may hold values from -4.5 to 4.5
- new_values: bfloat16 [128, 512], P(('grp', 'req')), parts along dimension 0, may hold values from -4.5 to 4.5
- cache_lengths: int32 [128], P(('grp', 'req')), parts along dimension 0, may hold values from 1 to 384
Outputs:
- moe_out: bfloat16 [512, 2048], P(('grp', 'req')), parts along dimension 0
- attention_out: bfloat16 [128, 4096], P(('grp', 'req')), parts along dimension 0
There are 2 independent parts, one for each index of `grp`. A program takes and returns all parts, laid end to end along the dimension named above; an argument that names none is the same for every part. Nothing has to cross between parts.
Inputs may be any that keep to these rules, and one draw needn't show every extreme that they name: `route_ids`: each row names 8 different experts; in each aligned block of 16 rows (the rows of one device) no expert is named by more than 16 rows, a bound that some block reaches.
All inputs are finite; a program needn't handle non-finite values.
Results may differ from a plain program's by a relative error of at most 0.0065.
Values may be sent and summed in bfloat16 or wider, within the bound.
A program may use at most 64 MiB of HBM per device.

v0:
```python
import jax
import jax.numpy as jnp
from jax import lax
from jax.sharding import PartitionSpec as P

EPS = 1e-06


def slot_table(route_ids, experts, capacity):
    onehot = (route_ids[:, :, None] == jnp.arange(experts, dtype=jnp.int32)[None, None, :]).astype(
        jnp.float32
    )
    present = jnp.sum(onehot, axis=1)
    earlier = jnp.cumsum(present, axis=0) - present
    levels = jnp.arange(capacity, dtype=jnp.float32)
    placed = present[:, :, None] * (earlier[:, :, None] == levels[None, None, :]).astype(
        jnp.float32
    )
    return (onehot, placed)


def expert_apply(received, w_gate, w_up, w_down):
    gate_part = jnp.einsum("nesd,edf->nesf", received, w_gate, preferred_element_type=jnp.float32)
    up_part = jnp.einsum("nesd,edf->nesf", received, w_up, preferred_element_type=jnp.float32)
    active = (jax.nn.silu(gate_part) * up_part).astype(jnp.bfloat16)
    return jnp.einsum("nesf,efd->nesd", active, w_down, preferred_element_type=jnp.float32).astype(
        jnp.bfloat16
    )


def attend(queries, keys_cache, values_cache, new_keys, new_values, cache_lengths):
    batch_rows = queries.shape[0]
    kv_heads = keys_cache.shape[1]
    cache_span = keys_cache.shape[2]
    head_size = keys_cache.shape[3]
    group_heads = queries.shape[1] // (kv_heads * head_size)
    score_scale = head_size ** (-0.5)
    grouped = queries.reshape(batch_rows, kv_heads, group_heads, head_size)
    scores = (
        jnp.einsum("bgqd,bgld->bgql", grouped, keys_cache, preferred_element_type=jnp.float32)
        * score_scale
    )
    own_score = (
        jnp.einsum(
            "bgqd,bgd->bgq",
            grouped,
            new_keys.reshape(batch_rows, kv_heads, head_size),
            preferred_element_type=jnp.float32,
        )
        * score_scale
    )
    live_mask = (jnp.arange(cache_span, dtype=jnp.int32)[None, :] < cache_lengths[:, None])[
        :, None, None, :
    ]
    highest = jnp.maximum(jnp.max(jnp.where(live_mask, scores, -jnp.inf), axis=-1), own_score)
    weights = jnp.where(live_mask, jnp.exp(scores - highest[..., None]), 0.0)
    own_weight = jnp.exp(own_score - highest)
    totals = jnp.sum(weights, axis=-1) + own_weight
    prob_low = (weights / totals[..., None]).astype(jnp.bfloat16)
    own_prob = (own_weight / totals).astype(jnp.bfloat16)
    mixed_out = jnp.einsum(
        "bgql,bgld->bgqd", prob_low, values_cache, preferred_element_type=jnp.float32
    )
    mixed_out = mixed_out + own_prob.astype(jnp.float32)[..., None] * new_values.reshape(
        batch_rows, kv_heads, 1, head_size
    ).astype(jnp.float32)
    return mixed_out.reshape(batch_rows, -1).astype(jnp.bfloat16)


def body(
    moe_input,
    norm_gain,
    route_ids,
    route_gates,
    expert_gate,
    expert_up,
    expert_down,
    queries,
    keys_cache,
    values_cache,
    new_keys,
    new_values,
    cache_lengths,
):
    row_count = moe_input.shape[0]
    model_width = moe_input.shape[1]
    local_experts = expert_gate.shape[0]
    devices = lax.axis_size("req")
    experts = devices * local_experts
    capacity = min(row_count, max(2, 16 * row_count // experts))
    hidden = moe_input.astype(jnp.float32)
    normed = (
        hidden
        * lax.rsqrt(jnp.mean(hidden * hidden, axis=-1, keepdims=True) + EPS)
        * norm_gain.astype(jnp.float32)
    ).astype(jnp.bfloat16)
    onehot, placed = slot_table(route_ids, experts, capacity)
    selector = placed.reshape(row_count, experts * capacity).astype(jnp.bfloat16)
    outgoing = jnp.einsum("rs,rd->sd", selector, normed, preferred_element_type=jnp.float32).astype(
        jnp.bfloat16
    )
    outgoing = outgoing.reshape(devices, local_experts, capacity, model_width)
    produced = expert_apply(
        lax.all_to_all(outgoing, "req", split_axis=0, concat_axis=0, tiled=True),
        expert_gate,
        expert_up,
        expert_down,
    )
    returned = lax.all_to_all(produced, "req", split_axis=0, concat_axis=0, tiled=True)
    weight = jnp.einsum("rke,rk->re", onehot, route_gates.astype(jnp.float32))
    combine = (
        (weight[:, :, None] * placed).reshape(row_count, experts * capacity).astype(jnp.bfloat16)
    )
    expert_sum = jnp.dot(
        combine,
        returned.reshape(experts * capacity, model_width),
        preferred_element_type=jnp.float32,
    )
    moe_out = (hidden + expert_sum).astype(jnp.bfloat16)
    attention_out = attend(queries, keys_cache, values_cache, new_keys, new_values, cache_lengths)
    return (moe_out, attention_out)


def solution(mesh):
    in_specs = (
        P(("grp", "req"), None),
        P(),
        P(("grp", "req"), None),
        P(("grp", "req"), None),
        P("req", None, None),
        P("req", None, None),
        P("req", None, None),
        P(("grp", "req"), None),
        P(("grp", "req"), None, None, None),
        P(("grp", "req"), None, None, None),
        P(("grp", "req"), None),
        P(("grp", "req"), None),
        P(("grp", "req")),
    )
    out_specs = (P(("grp", "req"), None), P(("grp", "req"), None))
    return jax.shard_map(body, mesh=mesh, in_specs=in_specs, out_specs=out_specs, check_vma=False)
```

profile of v0, /device:TPU:9, one launch (start us, length us, event | category | flops | bytes accessed | tf_op | source)
XLA Modules:
  0.0 79.7 jit_solution(15654762199548620591)
XLA Ops:
  0.6 0.0 copy-start
  0.6 0.0 copy-start.5
  0.7 0.9 %copy.19 = s32[16,8]{1,0:T(8,128)S(1)} copy(s32[16,8]{0,1:T(8,128)} %param.15) | data formatting | bytes 1024 | tf_op args[2]
  1.6 0.1 convert_reduce_fusion
  1.7 0.7 convert_element_type.81
  2.4 1.0 %fusion.38 = f32[16]{0:T(128)S(1)} fusion(bf16[16,2048]{1,0:T(8,128)(2,1)} %param.13), kind=kLoop, calls=%fused_computation.29 | loop fusion | flops 98288 | bytes 65600 | tf_op jit(solution)/shard_map/reduce_sum | solution.py:94
  3.4 0.1 mul.80
  3.5 0.1 mul.83
  3.6 0.1 eq.48
  3.7 0.1 eq.51
  3.8 0.1 eq.53
  3.9 2.4 %convolution_convert_fusion = bf16[256,2048]{1,0:T(8,128)(2,1)} fusion(bf16[16,2048]{1,0:T(8,128)(2,1)} %param.13, f32[2048]{0:T(1024)S(1)} %convert_element_type.81, f32[16]{0:T(128)S(1)} %add_rsqrt_fusion, bf16[16,256]{1,0:T(8,128)(2,1)S(1)} %mul.83, f32[16,256]{1,0:T(8,128)S(1)} %eq.51, f32[256]{0:T(256)S(1)} %eq.53), kind=kOutput, calls=%fused_computation.7 | convolution fusion | flops 17440768 | bytes 1147968 | tf_op jit(solution)/shard_map/rs,rd->sd/dot_general | solution.py:99
  6.3 6.6 %all-to-all-start = ((bf16[16,1,16,2048]{3,2,1,0:T(8,128)(2,1)}), bf16[16,1,16,2048]{3,2,1,0:T(8,128)(2,1)}, u32[]{:S(2)}, u32[]{:S(2)}) async-start(bf16[16,1,16,2048]{3,2,1,0:T(8,128)(2,1)} %bitcast.97), calls=%async_computation | async-start | bytes 2097152 | tf_op jit(solution)/shard_map/all_to_all | solution.py:104
  12.9 0.0 copy-done.5
  12.9 0.1 copy.22
  13.0 24.9 %all-to-all-done = bf16[16,1,16,2048]{3,2,1,0:T(8,128)(2,1)} async-done(((bf16[16,1,16,2048]{3,2,1,0:T(8,128)(2,1)}), bf16[16,1,16,2048]{3,2,1,0:T(8,128)(2,1)}, u32[]{:S(2)}, u32[]{:S(2)}) %all-to-all-start) | async-done | bytes 1048608 | tf_op jit(solution)/shard_map/all_to_all | solution.py:104
  37.8 4.1 %fusion.13 = f32[16,1,16,768]{3,2,0,1:T(8,128)} fusion(bf16[1,2048,768]{2,1,0:T(8,128)(2,1)} %param.17, bf16[16,1,16,2048]{3,2,1,0:T(8,128)(2,1)} %all-to-all-done), kind=kOutput, calls=%fused_computation.11 | convolution fusion | flops 805306368 | bytes 4980736 | tf_op jit(solution)/shard_map/nesd,edf->nesf/dot_general | solution.py:23
  41.9 0.0 copy-done
  41.9 0.0 copy-start.2
  42.0 5.6 %fusion.9 = bf16[16,1,16,2048]{3,2,1,0:T(8,128)(2,1)} fusion(bf16[1,768,2048]{2,1,0:T(8,128)(2,1)S(1)} %copy-done, bf16[1,2048,768]{2,1,0:T(8,128)(2,1)} %param.18, bf16[16,1,16,2048]{3,2,1,0:T(8,128)(2,1)} %all-to-all-done, f32[16,1,16,768]{3,2,0,1:T(8,128)} %fusion.13), kind=kOutput, calls=%fused_computation.8 | convolution fusion | flops 1612316672 | bytes 9175040 | tf_op jit(solution)/shard_map/nesf,efd->nesd/dot_general | solution.py:26
  47.5 5.1 %all-to-all-start.1 = ((bf16[16,1,16,2048]{3,2,1,0:T(8,128)(2,1)}), bf16[16,1,16,2048]{3,2,1,0:T(8,128)(2,1)}, u32[]{:S(2)}, u32[]{:S(2)}) async-start(bf16[16,1,16,2048]{3,2,1,0:T(8,128)(2,1)} %fusion.9), calls=%async_computation.1 | async-start | bytes 2097152 | tf_op jit(solution)/shard_map/all_to_all | solution.py:109
  52.6 0.2 fusion.48
  52.9 0.2 multiply_convert_fusion
  53.0 0.1 convert_element_type.79
  53.2 0.1 iota_compare_fusion.3
  53.3 0.1 fusion.49
  53.4 2.1 %select_reduce_fusion = (f32[4,4,8]{2,1,0:T(4,128)S(1)}, f32[4,4,8,384]{3,2,1,0:T(8,128)S(1)}) fusion(pred[4,384]{1,0:T(4,128)(4,1)S(1)} %iota_compare_fusion.3, bf16[4,4,384,128]{3,2,1,0:T(8,128)(2,1)} %param.21, bf16[1,4,32,128]{3,1,2,0:T(4,128)(2,1)S(1)} %bitcast.102), kind=kOutput, calls=%fused_computation.25 | convolution fusion | flops 12730240 | bytes 1804288 | tf_op jit(solution)/shard_map/bgqd,bgld->bgql/dot_general | solution.py:40
  55.6 0.2 fusion.37
  55.8 1.8 %fusion.29 = bf16[1,4,32,128]{3,2,1,0:T(8,128)(2,1)S(1)} fusion(bf16[4,4,384,128]{3,2,1,0:T(8,128)(2,1)} %param.22, f32[4,4,8,384]{3,2,1,0:T(8,128)S(1)} %get-tuple-element.5, f32[4,4,8]{2,1,0:T(4,128)S(1)} %get-tuple-element.3, f32[4,4,8]{2,1,0:T(4,128)S(1)} %multiply_maximum_fusion, pred[4,384]{1,0:T(4,128)(4,1)S(1)} %iota_compare_fusion.3, ...), kind=kOutput, calls=%fused_computation.19 | convolution fusion | flops 12828672 | bytes 1813504 | tf_op jit(solution)/shard_map/bgql,bgld->bgqd/dot_general | solution.py:61
  57.7 0.7 copy.39
  58.3 19.3 %all-to-all-done.1 = bf16[16,1,16,2048]{3,2,1,0:T(8,128)(2,1)} async-done(((bf16[16,1,16,2048]{3,2,1,0:T(8,128)(2,1)}), bf16[16,1,16,2048]{3,2,1,0:T(8,128)(2,1)}, u32[]{:S(2)}, u32[]{:S(2)}) %all-to-all-start.1) | async-done | bytes 1048608 | tf_op jit(solution)/shard_map/all_to_all | solution.py:109
  77.6 2.1 %fusion.12 = bf16[16,2048]{1,0:T(8,128)(2,1)} fusion(bf16[16,256]{1,0:T(8,128)(2,1)S(1)} %convert_element_type.79, bf16[256,2048]{1,0:T(8,128)(2,1)} %bitcast.25, bf16[16,2048]{1,0:T(8,128)(2,1)S(1)} %copy-done.1), kind=kOutput, calls=%fused_computation.10 | convolution fusion | flops 16875520 | bytes 1187840 | tf_op jit(solution)/shard_map/dot_general | solution.py:114
  (17 shorter events, 0.1 us)
Async XLA Ops:
  0.6 41.3 %copy-start = (bf16[1,768,2048]{2,1,0:T(8,128)(2,1)S(1)}, bf16[1,768,2048]{2,1,0:T(8,128)(2,1)}, u32[]{:S(2)}) copy-start(bf16[1,768,2048]{2,1,0:T(8,128)(2,1)} %param.19) | copy-start | bytes 9437188
  0.6 12.2 %copy-start.5 = (bf16[16,8]{0,1:T(8,128)(2,1)S(1)}, bf16[16,8]{0,1:T(8,128)(2,1)}, u32[]{:S(2)}) copy-start(bf16[16,8]{0,1:T(8,128)(2,1)} %param.16) | copy-start | bytes 772
  6.3 31.6 %all-to-all-start = ((bf16[16,1,16,2048]{3,2,1,0:T(8,128)(2,1)}), bf16[16,1,16,2048]{3,2,1,0:T(8,128)(2,1)}, u32[]{:S(2)}, u32[]{:S(2)}) async-start(bf16[16,1,16,2048]{3,2,1,0:T(8,128)(2,1)} %bitcast.97), calls=%async_computation | async-start | bytes 2097152 | tf_op jit(solution)/shard_map/all_to_all | solution.py:104
  41.9 11.2 %copy-start.3 = (bf16[4,512]{1,0:T(4,128)(2,1)S(1)}, bf16[4,512]{1,0:T(4,128)(2,1)}, u32[]{:S(2)}) copy-start(bf16[4,512]{1,0:T(4,128)(2,1)} %param.23) | copy-start | bytes 12292
  41.9 11.2 %copy-start.4 = (bf16[4,512]{1,0:T(4,128)(2,1)S(1)}, bf16[4,512]{1,0:T(4,128)(2,1)}, u32[]{:S(2)}) copy-start(bf16[4,512]{1,0:T(4,128)(2,1)} %param.24) | copy-start | bytes 12292
  41.9 11.3 %copy-start.6 = (s32[4]{0:T(128)S(1)}, s32[4]{0:T(128)}, u32[]{:S(2)}) copy-start(s32[4]{0:T(128)} %param.25) | copy-start | bytes 52
  41.9 11.3 %copy-start.2 = (bf16[4,4096]{1,0:T(4,128)(2,1)S(1)}, bf16[4,4096]{1,0:T(4,128)(2,1)}, u32[]{:S(2)}) copy-start(bf16[4,4096]{1,0:T(4,128)(2,1)} %param.20) | copy-start | bytes 98308
  47.5 30.1 %copy-start.1 = (bf16[16,2048]{1,0:T(8,128)(2,1)S(1)}, bf16[16,2048]{1,0:T(8,128)(2,1)}, u32[]{:S(2)}) copy-start(bf16[16,2048]{1,0:T(8,128)(2,1)} %param.13) | copy-start | bytes 196612
  47.5 30.1 %all-to-all-start.1 = ((bf16[16,1,16,2048]{3,2,1,0:T(8,128)(2,1)}), bf16[16,1,16,2048]{3,2,1,0:T(8,128)(2,1)}, u32[]{:S(2)}, u32[]{:S(2)}) async-start(bf16[16,1,16,2048]{3,2,1,0:T(8,128)(2,1)} %fusion.9), calls=%async_computation.1 | async-start | bytes 2097152 | tf_op jit(solution)/shard_map/all_to_all | solution.py:109
where the time goes:
time: 80.2 us; the launch traced here: 79.7 us
  waiting for transfers between devices  44.1 us (55%)
  matrix products  18.5 us (23%)
  starting transfers between devices  11.7 us (15%)
  local copies, waits for them, and re-layouts  2.34 us (3%)
  other arithmetic  2.27 us (3%)
    all_to_all x1, waiting for transfers between devices, body(): lax.all_to_all(outgoing, 'req', split_axis=0, concat_axis=0, tiled=True)  24.9 us
    all_to_all x1, waiting for transfers between devices, body(): lax.all_to_all(produced, 'req', split_axis=0, concat_axis=0, tiled=True)  19.3 us
    all_to_all x1, starting transfers between devices, body(): lax.all_to_all(outgoing, 'req', split_axis=0, concat_axis=0, tiled=True)  6.61 us
    dot_general x1, matrix products, expert_apply(): jnp.einsum('nesf,efd->nesd', active, w_down, preferred_element_type=jnp.f...  5.59 us
    all_to_all x1, starting transfers between devices, body(): lax.all_to_all(produced, 'req', split_axis=0, concat_axis=0, tiled=True)  5.1 us
    dot_general x1, matrix products, expert_apply(): jnp.einsum('nesd,edf->nesf', received, w_gate, preferred_element_type=jnp...  4.1 us
    dot_general x1, matrix products, body(): jnp.einsum('rs,rd->sd', selector, normed, preferred_element_type=jnp.floa...  2.35 us
    dot_general x1, matrix products, attend(): jnp.einsum('bgqd,bgld->bgql', grouped, keys_cache, preferred_element_type...  2.15 us
  transfers between devices with their start and end apart: 2, of which 2 were waited for; matrix products, arithmetic and copies ran while one was open for 7% of the time, Pallas kernels for 0%

commit v1 on v0

v1 whole, which is shorter than its diff:
```python
import functools
import jax
import jax.numpy as jnp
from jax import lax
from jax.experimental import pallas as pl
from jax.experimental.pallas import tpu as pltpu
from jax.sharding import PartitionSpec as P

EPS = 1e-06
F32 = jnp.float32
BF16 = jnp.bfloat16


def push(src, dst, send, recv, peer):
    copy = pltpu.make_async_remote_copy(
        src_ref=src,
        dst_ref=dst,
        send_sem=send,
        recv_sem=recv,
        device_id={"req": peer},
        device_id_type=pl.DeviceIdType.MESH,
    )
    copy.start()
    return copy


def kernel(
    n,
    moe_ref,
    gain_ref,
    ids_ref,
    gates_ref,
    wg_hbm,
    wu_hbm,
    wd_hbm,
    q_ref,
    k_hbm,
    v_hbm,
    nk_ref,
    nv_ref,
    len_ref,
    out_ref,
    att_ref,
    wg,
    wu,
    wd,
    kc,
    vc,
    rows,
    part,
    rcore,
    ry,
    total,
    rz,
    load_sem,
    zs,
    zr,
    ys,
    yr,
    cs,
    cr,
    bzs,
    bzr,
    bys,
    byr,
    bcs,
    bcr,
):
    block, width = moe_ref.shape
    local = wg.shape[0]
    far = n // 4
    half = n // 2
    lanes = rows.shape[-1] - width
    me = lax.axis_index("req")
    c, y, f = lax.rem(me, 2), lax.rem(me // 2, 2), me // 4
    sibling = me + 1 - 2 * c
    across = me + 2 - 4 * y

    def place(step):
        return lax.rem(f + step, far)

    def away(step):
        return place(step) * 4 + y * 2 + c

    loads = [
        pltpu.make_async_copy(src, dst, load_sem.at[i])
        for i, (src, dst) in enumerate(
            ((k_hbm, kc), (v_hbm, vc), (wg_hbm, wg), (wu_hbm, wu), (wd_hbm, wd))
        )
    ]
    for load in loads:
        load.start()

    barrier = pltpu.get_barrier_semaphore()
    for peer in [away(s) for s in range(1, far)] + [across, sibling]:
        pl.semaphore_signal(
            barrier, inc=1, device_id={"req": peer}, device_id_type=pl.DeviceIdType.MESH
        )

    hidden = moe_ref[...].astype(F32)
    scale = lax.rsqrt(jnp.mean(hidden * hidden, axis=-1, keepdims=True) + EPS)
    mine = y * far + f
    rows[c, mine, :, 0:width] = (hidden * scale * gain_ref[...].astype(F32)).astype(BF16)
    ids = ids_ref[...]
    gates = gates_ref[...].astype(F32)
    column = lax.broadcasted_iota(jnp.int32, (block, lanes), 1)
    weight = jnp.zeros((block, lanes), F32)
    for k in range(ids.shape[1]):
        weight = weight + jnp.where(column == ids[:, k : k + 1], gates[:, k : k + 1], 0.0)
    rows[c, mine, :, width:] = weight.astype(BF16)
    pl.semaphore_wait(barrier, far + 1)

    own = rows.at[c, mine]
    to_z = [push(own, own, zs.at[s], zr.at[s], away(s)) for s in range(1, far)]
    to_y = [push(own, own, ys.at[0], yr.at[0], across)]

    batch, heads, span, size = kc.shape
    group = q_ref.shape[1] // (heads * size)
    tall = group * batch
    root = size ** (-0.5)
    row_batch = lax.rem(lax.broadcasted_iota(jnp.int32, (tall, span), 0), batch)
    position = lax.broadcasted_iota(jnp.int32, (tall, span), 1)
    live = [(row_batch == b) & (position < len_ref[b]) for b in range(batch)]

    def attend(g):
        q = q_ref[:, g * group * size : (g + 1) * group * size].astype(F32)
        q = jnp.concatenate([q[:, h * size : (h + 1) * size] for h in range(group)], axis=0)
        nk = nk_ref[:, g * size : (g + 1) * size].astype(F32)
        nv = nv_ref[:, g * size : (g + 1) * size].astype(F32)
        nk = jnp.concatenate([nk] * group, axis=0)
        nv = jnp.concatenate([nv] * group, axis=0)
        own_score = jnp.sum(q * nk, axis=-1, keepdims=True) * root
        q = q.astype(BF16)
        scores = [
            lax.dot_general(
                q, kc[b, g], (((1,), (1,)), ((), ())), preferred_element_type=F32
            )
            * root
            for b in range(batch)
        ]
        top = own_score
        for b in range(batch):
            masked = jnp.where(live[b], scores[b], -jnp.inf)
            top = jnp.maximum(top, jnp.max(masked, axis=-1, keepdims=True))
        weights = [jnp.where(live[b], jnp.exp(scores[b] - top), 0.0) for b in range(batch)]
        own_weight = jnp.exp(own_score - top)
        totals = own_weight
        for b in range(batch):
            totals = totals + jnp.sum(weights[b], axis=-1, keepdims=True)
        mixed = (own_weight / totals).astype(BF16).astype(F32) * nv
        for b in range(batch):
            mixed = mixed + jnp.dot(
                (weights[b] / totals).astype(BF16), vc[b, g], preferred_element_type=F32
            )
        flat = [mixed[h * batch : (h + 1) * batch, :] for h in range(group)]
        att_ref[:, g * group * size : (g + 1) * group * size] = jnp.concatenate(
            flat, axis=1
        ).astype(BF16)

    loads[0].wait()
    loads[1].wait()
    first, second = (heads + 1) // 2, heads
    attend(0)
    for s in range(1, far):
        to_z[s - 1].wait_recv()
        got = rows.at[c, y * far + place(far - s)]
        to_y.append(push(got, got, ys.at[s], yr.at[s], across))
    near = rows.at[c, pl.ds(y * far, far)]
    to_core = [push(near, near, cs.at[0], cr.at[0], sibling)]
    for g in range(1, first):
        attend(g)
    for s in range(far):
        to_y[s].wait_recv()
    near = rows.at[c, pl.ds((1 - y) * far, far)]
    to_core.append(push(near, near, cs.at[1], cr.at[1], sibling))
    for load in loads[2:]:
        load.wait()

    step = min(half, 8)
    tile = 512 if width % 512 == 0 else width

    def experts(side):
        def chunk(i, carry):
            at = pl.ds(i * step, step)
            x = rows[side, at, :, 0:width].reshape(step * block, width)
            table = rows[side, at, :, width:].reshape(step * block, lanes).astype(F32)
            number = lax.broadcasted_iota(jnp.int32, table.shape, 1)
            active, chosen = [], []
            for e in range(local):
                gate = jnp.dot(x, wg[e], preferred_element_type=F32)
                up = jnp.dot(x, wu[e], preferred_element_type=F32)
                active.append((gate / (1.0 + jnp.exp(-gate)) * up).astype(BF16))
                picked = jnp.where(number == me * local + e, table, 0.0)
                chosen.append(jnp.sum(picked, axis=-1, keepdims=True))
            for t in range(0, width, tile):
                got = jnp.zeros((step * block, tile), F32)
                for e in range(local):
                    made = jnp.dot(active[e], wd[e, :, t : t + tile], preferred_element_type=F32)
                    got = got + chosen[e] * made.astype(BF16).astype(F32)
                part[side, at, :, t : t + tile] = got.astype(BF16).reshape(step, block, tile)
            return carry

        lax.fori_loop(0, half // step, chunk, 0)

    experts(c)
    to_core[0].wait_recv()
    to_core[1].wait_recv()
    experts(1 - c)

    back_core = push(part.at[1 - c], rcore, bcs, bcr, sibling)
    for g in range(first, second):
        attend(g)
    back_core.wait_recv()

    back_y = []
    for s in [*range(1, far), 0]:
        at = (1 - y) * far + place(s)
        part[c, at] = (part[c, at].astype(F32) + rcore[at].astype(F32)).astype(BF16)
        back_y.append(push(part.at[c, at], ry.at[s], bys.at[s], byr.at[s], across))
    back_z = []
    for s, arrived in zip([*range(1, far), 0], back_y):
        at = y * far + place(s)
        kept = part[c, at].astype(F32) + rcore[at].astype(F32)
        arrived.wait_recv()
        kept = kept + ry[s].astype(F32)
        if s:
            total[s - 1] = kept.astype(BF16)
            back_z.append(push(total.at[s - 1], rz.at[s - 1], bzs.at[s], bzr.at[s], away(s)))
    result = moe_ref[...].astype(F32) + kept
    for s in range(1, far):
        back_z[s - 1].wait_recv()
        result = result + rz[s - 1].astype(F32)
    out_ref[...] = result.astype(BF16)
    for copy in [*to_z, *to_y, *to_core, back_core, *back_y, *back_z]:
        copy.wait_send()


def body(*args):
    moe, gain, ids, gates, wg, wu, wd, q, k, v, nk, nv, lengths = args
    n = lax.axis_size("req")
    block, width = moe.shape
    experts = n * wg.shape[0]
    lanes = -(-experts // 128) * 128
    far, half = n // 4, n // 2
    vmem = pl.BlockSpec(memory_space=pltpu.VMEM)
    hbm = pl.BlockSpec(memory_space=pl.ANY)
    smem = pl.BlockSpec(memory_space=pltpu.SMEM)
    many = pltpu.SemaphoreType.DMA((far,))
    return pl.pallas_call(
        functools.partial(kernel, n),
        out_shape=(
            jax.ShapeDtypeStruct(moe.shape, BF16),
            jax.ShapeDtypeStruct(q.shape, BF16),
        ),
        in_specs=[vmem, vmem, vmem, vmem, hbm, hbm, hbm, vmem, hbm, hbm, vmem, vmem, smem],
        out_specs=(vmem, vmem),
        scratch_shapes=[
            pltpu.VMEM(wg.shape, BF16),
            pltpu.VMEM(wu.shape, BF16),
            pltpu.VMEM(wd.shape, BF16),
            pltpu.VMEM(k.shape, BF16),
            pltpu.VMEM(v.shape, BF16),
            pltpu.VMEM((2, half, block, width + lanes), BF16),
            pltpu.VMEM((2, half, block, width), BF16),
            pltpu.VMEM((half, block, width), BF16),
            pltpu.VMEM((far, block, width), BF16),
            pltpu.VMEM((far - 1, block, width), BF16),
            pltpu.VMEM((far - 1, block, width), BF16),
            pltpu.SemaphoreType.DMA((5,)),
            many,
            many,
            many,
            many,
            pltpu.SemaphoreType.DMA((2,)),
            pltpu.SemaphoreType.DMA((2,)),
            many,
            many,
            many,
            many,
            pltpu.SemaphoreType.DMA,
            pltpu.SemaphoreType.DMA,
        ],
        compiler_params=pltpu.CompilerParams(
            collective_id=0, has_side_effects=True, vmem_limit_bytes=58 * 1024 * 1024
        ),
    )(moe, gain.reshape(1, width), ids, gates, wg, wu, wd, q, k, v, nk, nv, lengths)


def solution(mesh):
    in_specs = (
        P(("grp", "req"), None),
        P(),
        P(("grp", "req"), None),
        P(("grp", "req"), None),
        P("req", None, None),
        P("req", None, None),
        P("req", None, None),
        P(("grp", "req"), None),
        P(("grp", "req"), None, None, None),
        P(("grp", "req"), None, None, None),
        P(("grp", "req"), None),
        P(("grp", "req"), None),
        P(("grp", "req")),
    )
    out_specs = (P(("grp", "req"), None), P(("grp", "req"), None))
    return jax.shard_map(body, mesh=mesh, in_specs=in_specs, out_specs=out_specs, check_vma=False)
```

time: 80.2 us -> 41.3 us (0.51)
  the two profiles are of different devices: /device:TPU:9 before, /device:TPU:0 now
where the time goes in v1:
time: 41.3 us; the launch traced here: 41 us
  Pallas kernels  33.5 us (81%)
  local copies, waits for them, and re-layouts  6.85 us (17%)
  between operations  0.64 us (2%)
    pallas_call x1, Pallas kernels, body(): pl.pallas_call(functools.partial(kernel, n), out_shape=(jax.ShapeDtypeStr...  33.5 us
    unnamed x4, local copies, waits for them, and re-layouts  5.56 us
    reshape x1, local copies, waits for them, and re-layouts, body(): gain.reshape(1, width)  1.29 us

profile of v1, /device:TPU:0, one launch (start us, length us, event | category | flops | bytes accessed | tf_op | source)
XLA Modules:
  0.0 41.0 jit_solution(13081182890902972663)
XLA Ops:
  0.6 1.3 %copy.16.gates_ref = bf16[16,8]{1,0:T(8,128)(2,1)} copy(bf16[16,8]{0,1:T(8,128)(2,1)} %param.16) | data formatting | bytes 512 | tf_op args[3]
  2.0 1.3 %reshape.7.gain_ref = bf16[1,2048]{1,0:T(2,128)(2,1)} reshape(bf16[2048]{0:T(1024)(128)(2,1)} %param.14) | data formatting | bytes 8192 | tf_op jit(solution)/shard_map/reshape | solution.py:286
  3.3 1.4 %copy.15.ids_ref = s32[16,8]{1,0:T(8,128)} copy(s32[16,8]{0,1:T(8,128)} %param.15) | data formatting | bytes 1024 | tf_op args[2]
  4.6 33.5 %shard_map.140 = (bf16[16,2048]{1,0:T(8,128)(2,1)}, bf16[4,4096]{1,0:T(4,128)(2,1)}) custom-call(bf16[16,2048]{1,0:T(8,128)(2,1)} %moe_ref.1, bf16[1,2048]{1,0:T(2,128)(2,1)} %reshape.7.gain_ref, s32[16,8]{1,0:T(8,128)} %copy.15.ids_ref, bf16[16,8]{1,0:T(8,128)(2,1)} %copy.16.gates_ref, bf16[1,2048,768]{2,1,0:T(8,128)(2,1)} %wg_hbm.1, ...), custom_call_target="tpu_custom_call" | custom-call | tf_op jit(solution)/shard_map/pallas_call | solution.py:249
  38.1 1.5 %copy.19 = bf16[16,2048]{1,0:T(8,128)(2,1)} copy(bf16[16,2048]{1,0:T(8,128)(2,1)} %get-tuple-element.4) | data formatting | bytes 131072
  39.6 1.4 %copy.20 = bf16[4,4096]{1,0:T(4,128)(2,1)} copy(bf16[4,4096]{1,0:T(4,128)(2,1)} %get-tuple-element.5) | data formatting | bytes 65536

commit v2 on v1

--- a/solution.py
+++ b/solution.py
@@ -11,8 +11,8 @@
 BF16 = jnp.bfloat16
 
 
-def push(src, dst, send, recv, peer):
-    copy = pltpu.make_async_remote_copy(
+def link(src, dst, send, recv, peer):
+    return pltpu.make_async_remote_copy(
         src_ref=src,
         dst_ref=dst,
         send_sem=send,
@@ -20,8 +20,31 @@
         device_id={"req": peer},
         device_id_type=pl.DeviceIdType.MESH,
     )
+
+
+def push(*args):
+    copy = link(*args)
     copy.start()
     return copy
+
+
+def flip(index, bit):
+    return index + bit - 2 * bit * lax.rem(index // bit, 2)
+
+
+def low_bit(offset):
+    return offset & -offset
+
+
+def spread(a_ref, b_ref, a_out, b_out, sem):
+    copies = [
+        pltpu.make_async_copy(a_ref, a_out, sem.at[0]),
+        pltpu.make_async_copy(b_ref, b_out, sem.at[1]),
+    ]
+    for copy in copies:
+        copy.start()
+    for copy in copies:
+        copy.wait()
 
 
 def kernel(
@@ -76,11 +99,20 @@
     sibling = me + 1 - 2 * c
     across = me + 2 - 4 * y
 
-    def place(step):
-        return lax.rem(f + step, far)
-
-    def away(step):
-        return place(step) * 4 + y * 2 + c
+    bits = [far >> (i + 1) for i in range(far.bit_length() - 1)]
+
+    def below(offset):
+        return [b for b in bits if not offset or b < low_bit(offset)]
+
+    def place(offset):
+        at = f
+        for b in bits:
+            if offset & b:
+                at = flip(at, b)
+        return at
+
+    def hop(bit):
+        return flip(f, bit) * 4 + y * 2 + c
 
     loads = [
         pltpu.make_async_copy(src, dst, load_sem.at[i])
@@ -92,7 +124,7 @@
         load.start()
 
     barrier = pltpu.get_barrier_semaphore()
-    for peer in [away(s) for s in range(1, far)] + [across, sibling]:
+    for peer in [hop(b) for b in bits] + [across, sibling]:
         pl.semaphore_signal(
             barrier, inc=1, device_id={"req": peer}, device_id_type=pl.DeviceIdType.MESH
         )
@@ -100,19 +132,35 @@
     hidden = moe_ref[...].astype(F32)
     scale = lax.rsqrt(jnp.mean(hidden * hidden, axis=-1, keepdims=True) + EPS)
     mine = y * far + f
-    rows[c, mine, :, 0:width] = (hidden * scale * gain_ref[...].astype(F32)).astype(BF16)
+    rows[c, mine, :, 0:width] = (hidden * scale * gain_ref[...].astype(F32).reshape(1, width)).astype(BF16)
     ids = ids_ref[...]
     gates = gates_ref[...].astype(F32)
-    column = lax.broadcasted_iota(jnp.int32, (block, lanes), 1)
-    weight = jnp.zeros((block, lanes), F32)
-    for k in range(ids.shape[1]):
-        weight = weight + jnp.where(column == ids[:, k : k + 1], gates[:, k : k + 1], 0.0)
-    rows[c, mine, :, width:] = weight.astype(BF16)
-    pl.semaphore_wait(barrier, far + 1)
-
-    own = rows.at[c, mine]
-    to_z = [push(own, own, zs.at[s], zr.at[s], away(s)) for s in range(1, far)]
-    to_y = [push(own, own, ys.at[0], yr.at[0], across)]
+    expert = lax.broadcasted_iota(jnp.int32, (lanes, block), 0)
+    weight = jnp.zeros((lanes, block), F32)
+    for k in range(ids.shape[0]):
+        weight = weight + jnp.where(expert == ids[k : k + 1, :], gates[k : k + 1, :], 0.0)
+    same = lax.broadcasted_iota(jnp.int32, (block, block), 0) == lax.broadcasted_iota(
+        jnp.int32, (block, block), 1
+    )
+    rows[c, mine, :, width:] = lax.dot_general(
+        same.astype(F32).astype(BF16),
+        weight.astype(BF16),
+        (((1,), (1,)), ((), ())),
+        preferred_element_type=F32,
+    ).astype(BF16)
+    pl.semaphore_wait(barrier, len(bits) + 2)
+
+    to_z, to_y, to_core = {}, {}, {}
+
+    def relay(offset):
+        got = rows.at[c, y * far + place(offset)]
+        for b in below(offset):
+            d = offset + b
+            to_z[d] = push(got, got, zs.at[d], zr.at[d], hop(b))
+        to_y[offset] = push(got, got, ys.at[offset], yr.at[offset], across)
+        to_core[offset] = push(got, got, cs.at[offset], cr.at[offset], sibling)
+
+    relay(0)
 
     batch, heads, span, size = kc.shape
     group = q_ref.shape[1] // (heads * size)
@@ -161,25 +209,34 @@
     loads[1].wait()
     first, second = (heads + 1) // 2, heads
     attend(0)
-    for s in range(1, far):
-        to_z[s - 1].wait_recv()
-        got = rows.at[c, y * far + place(far - s)]
-        to_y.append(push(got, got, ys.at[s], yr.at[s], across))
-    near = rows.at[c, pl.ds(y * far, far)]
-    to_core = [push(near, near, cs.at[0], cr.at[0], sibling)]
+    arrivals = sorted(range(1, far), key=lambda d: (-low_bit(d), d))
+    for d in arrivals:
+        to_z[d].wait_recv()
+        relay(d)
     for g in range(1, first):
         attend(g)
-    for s in range(far):
-        to_y[s].wait_recv()
-    near = rows.at[c, pl.ds((1 - y) * far, far)]
-    to_core.append(push(near, near, cs.at[1], cr.at[1], sibling))
+    for d in [0, *arrivals]:
+        to_y[d].wait_recv()
+        got = rows.at[c, (1 - y) * far + place(d)]
+        to_core[far + d] = push(got, got, cs.at[far + d], cr.at[far + d], sibling)
     for load in loads[2:]:
         load.wait()
 
     step = min(half, 8)
     tile = 512 if width % 512 == 0 else width
 
-    def experts(side):
+    def core_back(i, t):
+        at = pl.ds(i * step, step)
+        cut = pl.ds(t * tile, tile)
+        return link(
+            part.at[1 - c, at, :, cut],
+            rcore.at[at, :, cut],
+            bcs.at[i, t],
+            bcr.at[i, t],
+            sibling,
+        )
+
+    def experts(side, send):
         def chunk(i, carry):
             at = pl.ds(i * step, step)
             x = rows[side, at, :, 0:width].reshape(step * block, width)
@@ -198,40 +255,46 @@
                     made = jnp.dot(active[e], wd[e, :, t : t + tile], preferred_element_type=F32)
                     got = got + chosen[e] * made.astype(BF16).astype(F32)
                 part[side, at, :, t : t + tile] = got.astype(BF16).reshape(step, block, tile)
+                if send:
+                    core_back(i, t // tile).start()
             return carry
 
         lax.fori_loop(0, half // step, chunk, 0)
 
-    experts(c)
-    to_core[0].wait_recv()
-    to_core[1].wait_recv()
-    experts(1 - c)
-
-    back_core = push(part.at[1 - c], rcore, bcs, bcr, sibling)
+    experts(c, False)
+    for copy in to_core.values():
+        copy.wait_recv()
+    experts(1 - c, True)
+
     for g in range(first, second):
         attend(g)
-    back_core.wait_recv()
-
-    back_y = []
-    for s in [*range(1, far), 0]:
-        at = (1 - y) * far + place(s)
+    back_core = [core_back(i, t) for i in range(half // step) for t in range(width // tile)]
+    for copy in back_core:
+        copy.wait_recv()
+
+    back_y, back_z = {}, {}
+    for d in reversed(range(far)):
+        at = (1 - y) * far + place(d)
         part[c, at] = (part[c, at].astype(F32) + rcore[at].astype(F32)).astype(BF16)
-        back_y.append(push(part.at[c, at], ry.at[s], bys.at[s], byr.at[s], across))
-    back_z = []
-    for s, arrived in zip([*range(1, far), 0], back_y):
-        at = y * far + place(s)
+        back_y[d] = push(part.at[c, at], ry.at[d], bys.at[d], byr.at[d], across)
+    for d in reversed(range(far)):
+        at = y * far + place(d)
         kept = part[c, at].astype(F32) + rcore[at].astype(F32)
-        arrived.wait_recv()
-        kept = kept + ry[s].astype(F32)
-        if s:
-            total[s - 1] = kept.astype(BF16)
-            back_z.append(push(total.at[s - 1], rz.at[s - 1], bzs.at[s], bzr.at[s], away(s)))
-    result = moe_ref[...].astype(F32) + kept
-    for s in range(1, far):
-        back_z[s - 1].wait_recv()
-        result = result + rz[s - 1].astype(F32)
-    out_ref[...] = result.astype(BF16)
-    for copy in [*to_z, *to_y, *to_core, back_core, *back_y, *back_z]:
+        back_y[d].wait_recv()
+        kept = kept + ry[d].astype(F32)
+        for b in below(d):
+            back_z[d + b].wait_recv()
+            kept = kept + rz[d + b - 1].astype(F32)
+        if d:
+            total[d - 1] = kept.astype(BF16)
+            back_z[d] = push(
+                total.at[d - 1], rz.at[d - 1], bzs.at[d], bzr.at[d], hop(low_bit(d))
+            )
+    out_ref[...] = (moe_ref[...].astype(F32) + kept).astype(BF16)
+    for copies in (to_z, to_y, to_core, back_y, back_z):
+        for copy in copies.values():
+            copy.wait_send()
+    for copy in back_core:
         copy.wait_send()
 
 
@@ -246,7 +309,10 @@
     hbm = pl.BlockSpec(memory_space=pl.ANY)
     smem = pl.BlockSpec(memory_space=pltpu.SMEM)
     many = pltpu.SemaphoreType.DMA((far,))
-    return pl.pallas_call(
+    step = min(half, 8)
+    tile = 512 if width % 512 == 0 else width
+    pieces = pltpu.SemaphoreType.DMA((half // step, width // tile))
+    made = pl.pallas_call(
         functools.partial(kernel, n),
         out_shape=(
             jax.ShapeDtypeStruct(moe.shape, BF16),
@@ -271,19 +337,26 @@
             many,
             many,
             many,
-            pltpu.SemaphoreType.DMA((2,)),
-            pltpu.SemaphoreType.DMA((2,)),
-            many,
-            many,
-            many,
-            many,
-            pltpu.SemaphoreType.DMA,
-            pltpu.SemaphoreType.DMA,
+            pltpu.SemaphoreType.DMA((half,)),
+            pltpu.SemaphoreType.DMA((half,)),
+            many,
+            many,
+            many,
+            many,
+            pieces,
+            pieces,
         ],
         compiler_params=pltpu.CompilerParams(
             collective_id=0, has_side_effects=True, vmem_limit_bytes=58 * 1024 * 1024
         ),
-    )(moe, gain.reshape(1, width), ids, gates, wg, wu, wd, q, k, v, nk, nv, lengths)
+    )(moe, gain, ids.T, gates.T, wg, wu, wd, q, k, v, nk, nv, lengths)
+    return pl.pallas_call(
+        spread,
+        out_shape=tuple(jax.ShapeDtypeStruct(a.shape, a.dtype) for a in made),
+        in_specs=[hbm, hbm],
+        out_specs=(hbm, hbm),
+        scratch_shapes=[pltpu.SemaphoreType.DMA((2,))],
+    )(*made)
 
 
 def solution(mesh):

time: 41.3 us -> 38.3 us (0.927)
  local copies, waits for them, and re-layouts: 6.85 us -> 0 us
  Pallas kernels: 33.5 us -> 37.5 us
    unnamed x4 -> x0, local copies, waits for them, and re-layouts: 5.56 us -> none
    pallas_call x0 -> x1, Pallas kernels: none -> 4.1 us  [body(): pl.pallas_call(spread, out_shape=tuple((jax.ShapeDtypeStruct(a.shape, a.d...]
    reshape x1 -> x0, local copies, waits for them, and re-layouts: 1.29 us -> none  [body(): gain.reshape(1, width)]
where the time goes in v2:
time: 38.3 us; the launch traced here: 38.1 us
  Pallas kernels  37.5 us (98%)
  between operations  0.64 us (2%)
    pallas_call x1, Pallas kernels, body(): pl.pallas_call(functools.partial(kernel, n), out_shape=(jax.ShapeDtypeStr...  33.4 us
    pallas_call x1, Pallas kernels, body(): pl.pallas_call(spread, out_shape=tuple((jax.ShapeDtypeStruct(a.shape, a.d...  4.1 us

profile of v2, /device:TPU:0, one launch (start us, length us, event | category | flops | bytes accessed | tf_op | source)
XLA Modules:
  0.0 38.1 jit_solution(16294095172008194680)
XLA Ops:
  0.6 33.4 %shard_map.140 = (bf16[16,2048]{1,0:T(8,128)(2,1)}, bf16[4,4096]{1,0:T(4,128)(2,1)}) custom-call(bf16[16,2048]{1,0:T(8,128)(2,1)} %moe_ref.1, bf16[2048]{0:T(1024)(128)(2,1)} %gain_ref.1, s32[8,16]{1,0:T(8,128)} %bitcast.2, bf16[8,16]{1,0:T(8,128)(2,1)} %bitcast.3, bf16[1,2048,768]{2,1,0:T(8,128)(2,1)} %wg_hbm.1, bf16[1,2048,768]{2,1,0:T(8,128)(2,1)} %wu_hbm.1, ...), custom_call_target="tpu_custom_call" | custom-call | tf_op jit(solution)/shard_map/pallas_call | solution.py:315
  34.0 4.1 %shard_map.141 = (bf16[16,2048]{1,0:T(8,128)(2,1)}, bf16[4,4096]{1,0:T(4,128)(2,1)}) custom-call(bf16[16,2048]{1,0:T(8,128)(2,1)} %get-tuple-element.4.a_ref, bf16[4,4096]{1,0:T(4,128)(2,1)} %get-tuple-element.5.b_ref), custom_call_target="tpu_custom_call" | custom-call | tf_op jit(solution)/shard_map/pallas_call | solution.py:353

commit v3 on v2

--- a/solution.py
+++ b/solution.py
@@ -32,33 +32,28 @@
     return index + bit - 2 * bit * lax.rem(index // bit, 2)
 
 
-def low_bit(offset):
-    return offset & -offset
-
-
-def spread(a_ref, b_ref, a_out, b_out, sem):
-    copies = [
-        pltpu.make_async_copy(a_ref, a_out, sem.at[0]),
-        pltpu.make_async_copy(b_ref, b_out, sem.at[1]),
-    ]
-    for copy in copies:
-        copy.start()
-    for copy in copies:
-        copy.wait()
-
-
 def kernel(
     n,
+    moe_hbm,
+    gain_hbm,
+    ids_hbm,
+    gates_hbm,
+    wg_hbm,
+    wu_hbm,
+    wd_hbm,
+    q_hbm,
+    k_hbm,
+    v_hbm,
+    nk_hbm,
+    nv_hbm,
+    len_hbm,
+    out_hbm,
+    att_hbm,
     moe_ref,
     gain_ref,
     ids_ref,
     gates_ref,
-    wg_hbm,
-    wu_hbm,
-    wd_hbm,
     q_ref,
-    k_hbm,
-    v_hbm,
     nk_ref,
     nv_ref,
     len_ref,
@@ -75,6 +70,7 @@
     ry,
     total,
     rz,
+    small_sem,
     load_sem,
     zs,
     zr,
@@ -101,9 +97,6 @@
 
     bits = [far >> (i + 1) for i in range(far.bit_length() - 1)]
 
-    def below(offset):
-        return [b for b in bits if not offset or b < low_bit(offset)]
-
     def place(offset):
         at = f
         for b in bits:
@@ -111,8 +104,31 @@
                 at = flip(at, b)
         return at
 
-    def hop(bit):
-        return flip(f, bit) * 4 + y * 2 + c
+    def away(offset):
+        return place(offset) * 4 + y * 2 + c
+
+    small = [
+        pltpu.make_async_copy(src, dst, small_sem.at[i])
+        for i, (src, dst) in enumerate(
+            (
+                (moe_hbm, moe_ref),
+                (gain_hbm, gain_ref),
+                (ids_hbm, ids_ref),
+                (gates_hbm, gates_ref),
+                (q_hbm, q_ref),
+                (nk_hbm, nk_ref),
+                (nv_hbm, nv_ref),
+                (len_hbm, len_ref),
+            )
+        )
+    ]
+    for load in small:
+        load.start()
+    barrier = pltpu.get_barrier_semaphore()
+    for peer in [away(d) for d in range(1, far)] + [across, sibling]:
+        pl.semaphore_signal(
+            barrier, inc=1, device_id={"req": peer}, device_id_type=pl.DeviceIdType.MESH
+        )
 
     loads = [
         pltpu.make_async_copy(src, dst, load_sem.at[i])
@@ -123,12 +139,8 @@
     for load in loads:
         load.start()
 
-    barrier = pltpu.get_barrier_semaphore()
-    for peer in [hop(b) for b in bits] + [across, sibling]:
-        pl.semaphore_signal(
-            barrier, inc=1, device_id={"req": peer}, device_id_type=pl.DeviceIdType.MESH
-        )
-
+    for load in small[:4]:
+        load.wait()
     hidden = moe_ref[...].astype(F32)
     scale = lax.rsqrt(jnp.mean(hidden * hidden, axis=-1, keepdims=True) + EPS)
     mine = y * far + f
@@ -148,19 +160,20 @@
         (((1,), (1,)), ((), ())),
         preferred_element_type=F32,
     ).astype(BF16)
-    pl.semaphore_wait(barrier, len(bits) + 2)
+    pl.semaphore_wait(barrier, far + 1)
 
     to_z, to_y, to_core = {}, {}, {}
 
     def relay(offset):
         got = rows.at[c, y * far + place(offset)]
-        for b in below(offset):
-            d = offset + b
-            to_z[d] = push(got, got, zs.at[d], zr.at[d], hop(b))
+        for d in range(1, far) if offset == 0 else ():
+            to_z[d] = push(got, got, zs.at[d], zr.at[d], away(d))
         to_y[offset] = push(got, got, ys.at[offset], yr.at[offset], across)
         to_core[offset] = push(got, got, cs.at[offset], cr.at[offset], sibling)
 
     relay(0)
+    for load in small[4:]:
+        load.wait()
 
     batch, heads, span, size = kc.shape
     group = q_ref.shape[1] // (heads * size)
@@ -209,7 +222,7 @@
     loads[1].wait()
     first, second = (heads + 1) // 2, heads
     attend(0)
-    arrivals = sorted(range(1, far), key=lambda d: (-low_bit(d), d))
+    arrivals = range(1, far)
     for d in arrivals:
         to_z[d].wait_recv()
         relay(d)
@@ -268,6 +281,8 @@
 
     for g in range(first, second):
         attend(g)
+    att_copy = pltpu.make_async_copy(att_ref, att_hbm, small_sem.at[4])
+    att_copy.start()
     back_core = [core_back(i, t) for i in range(half // step) for t in range(width // tile)]
     for copy in back_core:
         copy.wait_recv()
@@ -282,20 +297,23 @@
         kept = part[c, at].astype(F32) + rcore[at].astype(F32)
         back_y[d].wait_recv()
         kept = kept + ry[d].astype(F32)
-        for b in below(d):
-            back_z[d + b].wait_recv()
-            kept = kept + rz[d + b - 1].astype(F32)
         if d:
             total[d - 1] = kept.astype(BF16)
-            back_z[d] = push(
-                total.at[d - 1], rz.at[d - 1], bzs.at[d], bzr.at[d], hop(low_bit(d))
-            )
-    out_ref[...] = (moe_ref[...].astype(F32) + kept).astype(BF16)
+            back_z[d] = push(total.at[d - 1], rz.at[d - 1], bzs.at[d], bzr.at[d], away(d))
+    kept = moe_ref[...].astype(F32) + kept
+    for d in range(1, far):
+        back_z[d].wait_recv()
+        kept = kept + rz[d - 1].astype(F32)
+    out_ref[...] = kept.astype(BF16)
+    out_copy = pltpu.make_async_copy(out_ref, out_hbm, small_sem.at[0])
+    out_copy.start()
     for copies in (to_z, to_y, to_core, back_y, back_z):
         for copy in copies.values():
             copy.wait_send()
     for copy in back_core:
         copy.wait_send()
+    att_copy.wait()
+    out_copy.wait()
 
 
 def body(*args):
@@ -305,22 +323,25 @@
     experts = n * wg.shape[0]
     lanes = -(-experts // 128) * 128
     far, half = n // 4, n // 2
-    vmem = pl.BlockSpec(memory_space=pltpu.VMEM)
     hbm = pl.BlockSpec(memory_space=pl.ANY)
-    smem = pl.BlockSpec(memory_space=pltpu.SMEM)
     many = pltpu.SemaphoreType.DMA((far,))
     step = min(half, 8)
     tile = 512 if width % 512 == 0 else width
     pieces = pltpu.SemaphoreType.DMA((half // step, width // tile))
-    made = pl.pallas_call(
+    small = (moe, gain, ids.T, gates.T, q, nk, nv)
+    return pl.pallas_call(
         functools.partial(kernel, n),
         out_shape=(
             jax.ShapeDtypeStruct(moe.shape, BF16),
             jax.ShapeDtypeStruct(q.shape, BF16),
         ),
-        in_specs=[vmem, vmem, vmem, vmem, hbm, hbm, hbm, vmem, hbm, hbm, vmem, vmem, smem],
-        out_specs=(vmem, vmem),
+        in_specs=[hbm] * 13,
+        out_specs=(hbm, hbm),
         scratch_shapes=[
+            *(pltpu.VMEM(a.shape, a.dtype) for a in small),
+            pltpu.SMEM(lengths.shape, lengths.dtype),
+            pltpu.VMEM(moe.shape, BF16),
+            pltpu.VMEM(q.shape, BF16),
             pltpu.VMEM(wg.shape, BF16),
             pltpu.VMEM(wu.shape, BF16),
             pltpu.VMEM(wd.shape, BF16),
@@ -332,6 +353,7 @@
             pltpu.VMEM((far, block, width), BF16),
             pltpu.VMEM((far - 1, block, width), BF16),
             pltpu.VMEM((far - 1, block, width), BF16),
+            pltpu.SemaphoreType.DMA((8,)),
             pltpu.SemaphoreType.DMA((5,)),
             many,
             many,
@@ -350,14 +372,6 @@
             collective_id=0, has_side_effects=True, vmem_limit_bytes=58 * 1024 * 1024
         ),
     )(moe, gain, ids.T, gates.T, wg, wu, wd, q, k, v, nk, nv, lengths)
-    return pl.pallas_call(
-        spread,
-        out_shape=tuple(jax.ShapeDtypeStruct(a.shape, a.dtype) for a in made),
-        in_specs=[hbm, hbm],
-        out_specs=(hbm, hbm),
-        scratch_shapes=[pltpu.SemaphoreType.DMA((2,))],
-    )(*made)
-
 
 def solution(mesh):
     in_specs = (

time: 38.3 us -> 36.1 us (0.943)
  Pallas kernels: 37.5 us -> 32.4 us
  local copies, waits for them, and re-layouts: 0 us -> 2.86 us
    pallas_call x1 -> x0, Pallas kernels: 4.1 us -> none  [body(): pl.pallas_call(spread, out_shape=tuple((jax.ShapeDtypeStruct(a.shape, a.d...]
    unnamed x0 -> x2, local copies, waits for them, and re-layouts: none -> 2.86 us
    pallas_call x1, Pallas kernels: 33.4 us -> 32.4 us  [body(): pl.pallas_call(functools.partial(kernel, n), out_shape=(jax.ShapeDtypeStr...]
where the time goes in v3:
time: 36.1 us; the launch traced here: 35.9 us
  Pallas kernels  32.4 us (90%)
  local copies, waits for them, and re-layouts  2.86 us (8%)
  between operations  0.64 us (2%)
    pallas_call x1, Pallas kernels, body(): pl.pallas_call(functools.partial(kernel, n), out_shape=(jax.ShapeDtypeStr...  32.4 us
    unnamed x2, local copies, waits for them, and re-layouts  2.86 us

profile of v3, /device:TPU:0, one launch (start us, length us, event | category | flops | bytes accessed | tf_op | source)
XLA Modules:
  0.0 35.9 jit_solution(6079747207351761521)
XLA Ops:
  0.6 32.4 %shard_map.140 = (bf16[16,2048]{1,0:T(8,128)(2,1)}, bf16[4,4096]{1,0:T(4,128)(2,1)}) custom-call(bf16[16,2048]{1,0:T(8,128)(2,1)} %moe_hbm.1, bf16[2048]{0:T(1024)(128)(2,1)} %gain_hbm.1, s32[8,16]{1,0:T(8,128)} %bitcast.2, bf16[8,16]{1,0:T(8,128)(2,1)} %bitcast.3, bf16[1,2048,768]{2,1,0:T(8,128)(2,1)} %wg_hbm.1, bf16[1,2048,768]{2,1,0:T(8,128)(2,1)} %wu_hbm.1, ...), custom_call_target="tpu_custom_call" | custom-call | tf_op jit(solution)/shard_map/pallas_call | solution.py:332
  33.0 1.5 %copy.17 = bf16[16,2048]{1,0:T(8,128)(2,1)} copy(bf16[16,2048]{1,0:T(8,128)(2,1)} %get-tuple-element.4) | data formatting | bytes 131072
  34.5 1.4 %copy.18 = bf16[4,4096]{1,0:T(4,128)(2,1)} copy(bf16[4,4096]{1,0:T(4,128)(2,1)} %get-tuple-element.5) | data formatting | bytes 65536
